TPU v7x, 32 devices: a whole 2x2x4 slice. The times are simulated.
32 devices in a mesh: band: 32 (over z, y, x, core).
Axes of the slice: x: 2, y: 2, z: 4, core: 2. Of those that a mesh axis runs over, the one named last changes fastest.
Arguments:
- grid_input: bfloat16 [227, 32768], P(None, 'band'), may hold values from -6 to 6
- mesh_init: bfloat16 [8192, 512], P('band'), may hold values from -6 to 6
- cotangent: bfloat16 [8192, 512], P('band'), may hold values from -6 to 6
- grid_lists: int32 [64, 256], P('band'), may hold values from 0 to 1023
- encoder_source: int32 [49152], P('band'), may hold values from 0 to 1535
- encoder_target: int32 [49152], P('band'), may hold values from 0 to 255
- mesh_lists: int32 [1024, 2], P('band'), may hold values from 0 to 255
- mesh_source: int32 [65536], P('band'), may hold values from 0 to 319
- mesh_target: int32 [65536], P('band'), may hold values from 0 to 255
- w_embed: bfloat16 [227, 512], replicated, may hold values from -0.375 to 0.375
- w_source: bfloat16 [512, 512], replicated, may hold values from -0.25 to 0.25
- w_target: bfloat16 [512, 512], replicated, may hold values from -0.25 to 0.25
- w_node: bfloat16 [512, 512], replicated, may hold values from -0.109375 to 0.109375
- w_sender: bfloat16 [512, 512], replicated, may hold values from -0.25 to 0.25
- w_receiver: bfloat16 [512, 512], replicated, may hold values from -0.25 to 0.25
- w_update: bfloat16 [512, 512], replicated, may hold values from -0.09375 to 0.09375
Outputs:
- mesh_out: bfloat16 [8192, 512], P('band')
- grad_grid: bfloat16 [227, 32768], P(None, 'band')
- grad_mesh: bfloat16 [8192, 512], P('band')
Inputs may be any that keep to these rules, and one draw needn't show every extreme that they name: `grid_lists`: local grid row of the sending band. `encoder_source`: row of the band's grid source table. `mesh_lists`: local mesh node of the sending patch. `mesh_source`: row of the patch's mesh source table.
All inputs are finite; a program needn't handle non-finite values.
Results may differ from a plain program's by a relative error of at most 0.025.
Values may be sent and summed in bfloat16 or wider, within the bound.
A program may use at most 128 MiB of HBM per device.

v0:
```python
import jax
import jax.numpy as jnp
from jax import lax
from jax.sharding import PartitionSpec as P


def padded(block, sides, width):
    for axis, dim in sides:
        count = lax.axis_size(axis)
        forward = [(i, i + 1) for i in range(count - 1)]
        backward = [(target, source) for source, target in forward]
        low = lax.ppermute(
            lax.slice_in_dim(block, block.shape[dim] - width, None, axis=dim), axis, forward
        )
        high = lax.ppermute(lax.slice_in_dim(block, 0, width, axis=dim), axis, backward)
        block = jnp.concatenate([low, block, high], axis=dim)
    return block


def rounded(values):
    return lax.optimization_barrier(values.astype(jnp.bfloat16)).astype(jnp.float32)


def indicator(indices, count):
    return (indices[:, None] == jnp.arange(count, dtype=jnp.int32)[None, :]).astype(jnp.bfloat16)


def carry_rows(selector, values, axis):
    high = values.astype(jnp.bfloat16)
    low = (values - high.astype(jnp.float32)).astype(jnp.bfloat16)
    dims = (((axis,), (0,)), ((), ()))
    first = lax.dot_general(selector, high, dims, preferred_element_type=jnp.float32)
    return first + lax.dot_general(selector, low, dims, preferred_element_type=jnp.float32)


def local(
    grid_input,
    mesh_init,
    cotangent,
    grid_lists,
    encoder_source,
    encoder_target,
    mesh_lists,
    mesh_source,
    mesh_target,
    w_embed,
    w_source,
    w_target,
    w_node,
    w_sender,
    w_receiver,
    w_update,
):
    band_count = lax.axis_size("band")
    grid_count = grid_input.shape[1]
    node_count = mesh_init.shape[0]
    latent_width = mesh_init.shape[1]
    grid_slots = grid_lists.shape[1]
    mesh_slots = mesh_lists.shape[1]

    def embedding(grid_values):
        hidden = jax.nn.silu(
            lax.dot_general(
                grid_values, w_embed, (((0,), (0,)), ((), ())), preferred_element_type=jnp.float32
            )
        ).astype(jnp.bfloat16)
        return rounded(jnp.dot(hidden, w_source, preferred_element_type=jnp.float32))

    source_rows, embed_pull = jax.vjp(embedding, grid_input)
    source_half = source_rows.astype(jnp.bfloat16)
    list_rows = jnp.concatenate([grid_lists[0], grid_lists[1]], axis=0)
    list_select = indicator(list_rows, grid_count)
    outgoing = jnp.dot(list_select, source_half, preferred_element_type=jnp.float32).astype(
        jnp.bfloat16
    )
    extended = padded(outgoing, (("band", 0),), grid_slots)
    grid_table = jnp.concatenate(
        [source_half, extended[:grid_slots], extended[3 * grid_slots :]], axis=0
    )
    source_select = indicator(encoder_source, grid_table.shape[0])
    edge_source = jnp.dot(source_select, grid_table, preferred_element_type=jnp.float32)
    enc_onehot = (
        jnp.arange(node_count, dtype=jnp.int32)[:, None] == encoder_target[None, :]
    ).astype(jnp.bfloat16)
    proc_onehot = (jnp.arange(node_count, dtype=jnp.int32)[:, None] == mesh_target[None, :]).astype(
        jnp.bfloat16
    )
    mesh_float = mesh_init.astype(jnp.float32)

    def target_side(mesh_values):
        return jnp.dot(
            mesh_values.astype(jnp.bfloat16), w_target, preferred_element_type=jnp.float32
        )

    target_proj, target_pull = jax.vjp(target_side, mesh_float)
    edge_target = carry_rows(enc_onehot, target_proj, 0)

    def encoder(source_values, target_values, mesh_values):
        message = jax.nn.silu(source_values + target_values).astype(jnp.bfloat16)
        summed = jnp.dot(enc_onehot, message, preferred_element_type=jnp.float32)
        return rounded(
            mesh_values
            + jax.nn.silu(
                jnp.dot(summed.astype(jnp.bfloat16), w_node, preferred_element_type=jnp.float32)
            )
        )

    latent, encode_pull = jax.vjp(encoder, edge_source, edge_target, mesh_float)

    def projection(latent_values):
        return rounded(
            jnp.dot(
                latent_values.astype(jnp.bfloat16), w_sender, preferred_element_type=jnp.float32
            )
        )

    sender_rows, project_pull = jax.vjp(projection, latent)
    sender_half = sender_rows.astype(jnp.bfloat16)
    flat_lists = mesh_lists.reshape(-1)
    mesh_select = indicator(flat_lists, node_count)
    outbound = jnp.dot(mesh_select, sender_half, preferred_element_type=jnp.float32).astype(
        jnp.bfloat16
    )
    outbound = outbound.reshape(band_count, mesh_slots, latent_width)
    received = lax.all_to_all(outbound, "band", split_axis=0, concat_axis=0, tiled=True)
    received = received.reshape(band_count * mesh_slots, latent_width)
    mesh_table = jnp.concatenate([sender_half, received], axis=0)
    proc_select = indicator(mesh_source, mesh_table.shape[0])
    edge_sender = jnp.dot(proc_select, mesh_table, preferred_element_type=jnp.float32)

    def receiver_side(latent_values):
        return jnp.dot(
            latent_values.astype(jnp.bfloat16), w_receiver, preferred_element_type=jnp.float32
        )

    receiver_proj, receiver_pull = jax.vjp(receiver_side, latent)
    edge_receiver = carry_rows(proc_onehot, receiver_proj, 0)

    def processor(sender_values, receiver_values, latent_values):
        message = jax.nn.silu(sender_values + receiver_values).astype(jnp.bfloat16)
        summed = jnp.dot(proc_onehot, message, preferred_element_type=jnp.float32)
        update = jax.nn.silu(
            jnp.dot(summed.astype(jnp.bfloat16), w_update, preferred_element_type=jnp.float32)
        )
        return (latent_values + update).astype(jnp.bfloat16)

    mesh_out, process_pull = jax.vjp(processor, edge_sender, edge_receiver, latent)
    grad_edge_sender, grad_edge_receiver, grad_latent_direct = process_pull(cotangent)
    grad_table = carry_rows(proc_select, grad_edge_sender, 0)
    (grad_latent_receiver,) = receiver_pull(carry_rows(proc_onehot, grad_edge_receiver, 1))
    grad_received = grad_table[node_count:].reshape(band_count, mesh_slots, latent_width)
    returned_mesh = lax.all_to_all(
        grad_received.astype(jnp.bfloat16), "band", split_axis=0, concat_axis=0, tiled=True
    ).astype(grad_received.dtype)
    grad_sender = grad_table[:node_count] + carry_rows(
        mesh_select, returned_mesh.reshape(-1, latent_width), 0
    )
    (grad_latent_project,) = project_pull(grad_sender)
    grad_latent = grad_latent_direct + grad_latent_receiver + grad_latent_project
    grad_edge_source, grad_edge_target, grad_mesh_direct = encode_pull(grad_latent)
    (grad_mesh_target,) = target_pull(carry_rows(enc_onehot, grad_edge_target, 1))
    grad_mesh = (grad_mesh_direct + grad_mesh_target).astype(jnp.bfloat16)
    grad_grid_table = carry_rows(source_select, grad_edge_source, 0)
    grad_from_lower = grad_grid_table[grid_count : grid_count + grid_slots]
    grad_from_upper = grad_grid_table[grid_count + grid_slots :]
    returned_grid = padded(
        jnp.concatenate([grad_from_lower, grad_from_upper], axis=0).astype(jnp.bfloat16),
        (("band", 0),),
        grid_slots,
    ).astype(jnp.float32)
    grad_lists = jnp.concatenate(
        [returned_grid[:grid_slots], returned_grid[3 * grid_slots :]], axis=0
    )
    grad_source = grad_grid_table[:grid_count] + carry_rows(list_select, grad_lists, 0)
    (grad_grid,) = embed_pull(grad_source)
    return (mesh_out, grad_grid, grad_mesh)


def solution(mesh):
    placed = (
        P(None, "band"),
        P("band", None),
        P("band", None),
        P("band", None),
        P("band"),
        P("band"),
        P("band", None),
        P("band"),
        P("band"),
        P(),
        P(),
        P(),
        P(),
        P(),
        P(),
        P(),
    )
    return jax.shard_map(
        local,
        mesh=mesh,
        in_specs=placed,
        out_specs=(P("band", None), P(None, "band"), P("band", None)),
        check_vma=False,
    )
```

profile of v0, /device:TPU:7, one launch (start us, length us, event | category | flops | bytes accessed | tf_op | source)
XLA Modules:
  0.0 114.0 jit_solution(3436869665179691860)
XLA Ops:
  0.6 0.8 fusion.140
  1.4 1.6 %fusion.142 = f32[1024,512]{1,0:T(8,128)S(1)} fusion(bf16[227,1024]{1,0:T(8,128)(2,1)} %param.16, bf16[227,512]{1,0:T(8,128)(2,1)} %param.25), kind=kOutput, calls=%fused_computation.171 | convolution fusion | flops 238026752 | bytes 2794496 | tf_op jit(solution)/shard_map/jvp()/dot_general | solution.py:63
  3.0 2.1 %convolution_convert_fusion.3 = bf16[1024,512]{1,0:T(8,128)(2,1)S(1)} fusion(bf16[512,512]{1,0:T(8,128)(2,1)} %param.26, f32[1024,512]{1,0:T(8,128)S(1)} %fusion.142), kind=kOutput, calls=%fused_computation.66 | convolution fusion | flops 540016640 | bytes 3670016 | tf_op jit(solution)/shard_map/jvp()/dot_general | solution.py:67
  5.2 0.8 fusion.40
  6.0 3.7 %collective-permute-start = (bf16[256,512]{1,0:T(8,128)(2,1)S(1)}, bf16[256,512]{1,0:T(8,128)(2,1)S(1)}, u32[]{:S(2)}, u32[]{:S(2)}) collective-permute-start(bf16[256,512]{1,0:T(8,128)(2,1)S(1)} %get-tuple-element.7), channel_id=1, source_target_pairs={{0,1},{1,2},{2,3},{3,4},{4,5},{5,6},{6,7},{7,8},{8,9},{9,10},{10,1... | collective-permute-start | bytes 786440 | tf_op jit(solution)/shard_map/ppermute | solution.py:12
  9.7 1.9 %collective-permute-start.1 = (bf16[256,512]{1,0:T(8,128)(2,1)S(1)}, bf16[256,512]{1,0:T(8,128)(2,1)S(1)}, u32[]{:S(2)}, u32[]{:S(2)}) collective-permute-start(bf16[256,512]{1,0:T(8,128)(2,1)S(1)} %get-tuple-element.8), channel_id=1, source_target_pairs={{1,0},{2,1},{3,2},{4,3},{5,4},{6,5},{7,6},{8,7},{9,8},{10,9},{11,1... | collective-permute-start | bytes 786440 | tf_op jit(solution)/shard_map/ppermute | solution.py:15
  11.8 0.1 eq.95
  11.9 0.3 fusion.143
  12.2 0.6 fusion.39
  12.9 0.6 convolution_add_fusion
  13.5 5.7 %collective-permute-done.1 = bf16[256,512]{1,0:T(8,128)(2,1)S(1)} collective-permute-done((bf16[256,512]{1,0:T(8,128)(2,1)S(1)}, bf16[256,512]{1,0:T(8,128)(2,1)S(1)}, u32[]{:S(2)}, u32[]{:S(2)}) %collective-permute-start.1) | collective-permute-done | bytes 262176 | tf_op jit(solution)/shard_map/ppermute | solution.py:15
  19.2 4.5 %fusion.8 = f32[1536,512]{1,0:T(8,128)} fusion(f32[1536,512]{1,0:T(8,128)S(1)} %convolution_add_fusion, s32[1536]{0:T(1024)S(1)} %copy-done.23, bf16[256,512]{1,0:T(8,128)(2,1)S(1)} %collective-permute-done.1, bf16[256,512]{1,0:T(8,128)(2,1)S(1)} %collective-permute-done, bf16[1024,512]{1,0:T(8,128)(2,1)S(1)} %copy-done.26), kind=kOutput, calls=%fused_computation.20 | convolution fusion | flops 2423783424 | bytes 7870464 | tf_op jit(solution)/shard_map/dot_general | solution.py:81
  23.7 4.1 %add_convert_fusion.1 = (bf16[256,512]{1,0:T(8,128)(2,1)S(1)}, f32[256,512]{1,0:T(8,128)}) fusion(bf16[256,512]{1,0:T(8,128)(2,1)S(1)} %copy-done.10, bf16[512,512]{1,0:T(8,128)(2,1)S(1)} %copy-done.22, f32[1536,512]{1,0:T(8,128)} %fusion.8, s32[1536]{0:T(1024)S(1)} %copy-done.14), kind=kOutput, calls=%fused_computation.129 | convolution fusion | flops 542244864 | bytes 4724736 | tf_op jit(solution)/shard_map/jvp()/dot_general | solution.py:104
  27.8 0.3 convolution_convert_fusion.5
  28.2 0.2 convolution_convert_fusion.8
  28.4 0.7 reshape.26
  29.0 4.8 %all-to-all-start = ((bf16[32,2,512]{2,1,0:T(2,128)(2,1)}), bf16[32,2,512]{2,1,0:T(2,128)(2,1)S(1)}, u32[]{:S(2)}, u32[]{:S(2)}) async-start(bf16[32,2,512]{2,1,0:T(2,128)(2,1)} %reshape.26), calls=%async_computation | async-start | bytes 131072 | tf_op jit(solution)/shard_map/all_to_all | solution.py:125
  33.9 0.3 fusion.144
  34.2 2.7 %fusion.24 = f32[2048,512]{1,0:T(8,128)} fusion(s32[2048]{0:T(1024)S(1)} %copy-done.15, f32[256,512]{1,0:T(8,128)S(1)} %fusion.144), kind=kOutput, calls=%fused_computation.45 | convolution fusion | flops 537526272 | bytes 4726784 | tf_op jit(solution)/shard_map/dot_general | solution.py:32
  36.9 2.2 %all-to-all-done = bf16[32,2,512]{2,1,0:T(2,128)(2,1)S(1)} async-done(((bf16[32,2,512]{2,1,0:T(2,128)(2,1)}), bf16[32,2,512]{2,1,0:T(2,128)(2,1)S(1)}, u32[]{:S(2)}, u32[]{:S(2)}) %all-to-all-start) | async-done | bytes 65568 | tf_op jit(solution)/shard_map/all_to_all | solution.py:125
  39.2 1.3 %fusion.14 = f32[2048,512]{1,0:T(8,128)S(1)} fusion(s32[2048]{0:T(1024)S(1)} %copy-done.13, bf16[64,512]{1,0:T(8,128)(2,1)S(1)} %reshape.27, bf16[256,512]{1,0:T(8,128)(2,1)S(1)} %convolution_convert_fusion.5), kind=kOutput, calls=%fused_computation.29 | convolution fusion | flops 672399360 | bytes 4530176 | tf_op jit(solution)/shard_map/dot_general | solution.py:129
  40.5 0.9 copy-done.2
  41.4 2.8 %add_add_fusion = f32[2048,512]{1,0:T(8,128)} fusion(f32[2048,512]{1,0:T(8,128)S(1)} %fusion.14, f32[2048,512]{1,0:T(8,128)S(1)} %copy-done.2, s32[2048]{0:T(1024)S(1)} %copy-done.15, f32[256,512]{1,0:T(8,128)S(1)} %fusion.144), kind=kOutput, calls=%fused_computation.16 | convolution fusion | flops 540016640 | bytes 13115392 | tf_op jit(solution)/shard_map/dot_general | solution.py:33
  44.2 4.7 %add_convert_fusion = (bf16[256,512]{1,0:T(8,128)(2,1)}, f32[256,512]{1,0:T(8,128)S(1)}) fusion(bf16[256,512]{1,0:T(8,128)(2,1)S(1)} %get-tuple-element.11, bf16[512,512]{1,0:T(8,128)(2,1)S(1)} %copy-done, f32[2048,512]{1,0:T(8,128)} %add_add_fusion, s32[2048]{0:T(1024)S(1)} %copy-done.16), kind=kOutput, calls=%fused_computation.126 | convolution fusion | flops 677904384 | bytes 5775360 | tf_op jit(solution)/shard_map/jvp()/dot_general | solution.py:143
  48.9 6.3 %fusion.6 = f32[2048,512]{1,0:T(8,128)} fusion(f32[2048,512]{1,0:T(8,128)} %add_add_fusion, bf16[512,512]{1,0:T(8,128)(2,1)S(1)} %copy-done, s32[2048]{0:T(1024)S(1)} %copy-done.16, bf16[256,512]{1,0:T(8,128)(2,1)S(1)} %copy-done.11, f32[256,512]{1,0:T(8,128)S(1)} %get-tuple-element.14), kind=kOutput, calls=%fused_computation.11 | convolution fusion | flops 684589056 | bytes 9707520 | tf_op jit(solution)/shard_map/transpose(jvp())/dot_general | solution.py:141
  55.2 5.1 %fusion.21 = f32[256,512]{1,0:T(8,128)} fusion(s32[2048]{0:T(1024)S(1)} %copy-done.16, f32[2048,512]{1,0:T(8,128)} %fusion.6), kind=kOutput, calls=%fused_computation.42 | convolution fusion | flops 541589504 | bytes 4726784 | tf_op jit(solution)/shard_map/dot_general | solution.py:33
  60.3 1.5 %fusion.12 = f32[320,512]{1,0:T(8,128)S(1)} fusion(s32[2048]{0:T(1024)S(1)} %copy-done.13, f32[2048,512]{1,0:T(8,128)S(1)} %copy-done.1), kind=kOutput, calls=%fused_computation.27 | convolution fusion | flops 675938304 | bytes 4857856 | tf_op jit(solution)/shard_map/dot_general | solution.py:33
  61.8 1.5 %fusion.44 = f32[320,512]{1,0:T(8,128)S(1)} fusion(f32[320,512]{1,0:T(8,128)S(1)} %fusion.12, s32[2048]{0:T(1024)S(1)} %copy-done.13, f32[2048,512]{1,0:T(8,128)S(1)} %copy-done.1), kind=kOutput, calls=%fused_computation.69 | convolution fusion | flops 672956416 | bytes 5513216 | tf_op jit(solution)/shard_map/dot_general | solution.py:32
  63.3 0.7 convert_element_type.215
  63.9 5.3 %all-to-all-start.1 = ((bf16[32,2,512]{2,1,0:T(2,128)(2,1)}), bf16[32,2,512]{2,1,0:T(2,128)(2,1)}, u32[]{:S(2)}, u32[]{:S(2)}) async-start(bf16[32,2,512]{2,1,0:T(2,128)(2,1)} %convert_element_type.215), calls=%async_computation.1 | async-start | bytes 131072 | tf_op jit(solution)/shard_map/all_to_all | solution.py:152
  69.2 3.2 %fusion.64 = f32[256,512]{1,0:T(8,128)S(1)} fusion(bf16[512,512]{1,0:T(8,128)(2,1)S(1)} %copy-done.4, f32[256,512]{1,0:T(8,128)} %fusion.21, s32[2048]{0:T(1024)} %param.24, bf16[256,512]{1,0:T(8,128)(2,1)S(1)} %copy-done.11, f32[2048,512]{1,0:T(8,128)} %fusion.6), kind=kOutput, calls=%fused_computation.90 | convolution fusion | flops 673316864 | bytes 6037504 | tf_op jit(solution)/shard_map/transpose(jvp())/dot_general | solution.py:132
  72.5 2.2 %all-to-all-done.1 = bf16[32,2,512]{2,1,0:T(2,128)(2,1)} async-done(((bf16[32,2,512]{2,1,0:T(2,128)(2,1)}), bf16[32,2,512]{2,1,0:T(2,128)(2,1)}, u32[]{:S(2)}, u32[]{:S(2)}) %all-to-all-start.1) | async-done | bytes 65568 | tf_op jit(solution)/shard_map/all_to_all | solution.py:152
  74.7 0.9 reshape.28
  75.6 0.3 fusion.114
  75.9 0.3 fusion.65
  76.2 0.3 fusion.60
  76.6 5.6 %fusion.10 = f32[1536,512]{1,0:T(8,128)} fusion(f32[1536,512]{1,0:T(8,128)} %fusion.8, bf16[512,512]{1,0:T(8,128)(2,1)} %param.28, s32[1536]{0:T(1024)S(1)} %copy-done.14, bf16[256,512]{1,0:T(8,128)(2,1)S(1)} %fusion.60, f32[256,512]{1,0:T(8,128)} %get-tuple-element.12), kind=kOutput, calls=%fused_computation.22 | convolution fusion | flops 547356672 | bytes 7608320 | tf_op jit(solution)/shard_map/transpose(jvp())/dot_general | solution.py:100
  82.2 3.6 %fusion.36 = f32[256,512]{1,0:T(8,128)S(1)} fusion(s32[1536]{0:T(1024)S(1)} %copy-done.14, f32[1536,512]{1,0:T(8,128)} %fusion.10), kind=kOutput, calls=%fused_computation.61 | convolution fusion | flops 406192128 | bytes 3676160 | tf_op jit(solution)/shard_map/dot_general | solution.py:33
  85.7 0.2 copy-done.3
  85.9 3.1 %fusion = f32[1536,512]{1,0:T(8,128)S(1)} fusion(s32[1536]{0:T(1024)S(1)} %copy-done.24, f32[1536,512]{1,0:T(8,128)S(1)} %copy-done.3), kind=kOutput, calls=%fused_computation.1 | convolution fusion | flops 2421424128 | bytes 6297600 | tf_op jit(solution)/shard_map/dot_general | solution.py:33
  89.0 4.9 %fusion.141 = (bf16[1536,512]{1,0:T(8,128)(2,1)S(1)}, f32[1536,512]{1,0:T(8,128)}) fusion(f32[1536,512]{1,0:T(8,128)S(1)} %fusion, f32[1536,512]{1,0:T(8,128)S(1)} %copy-done.3, s32[1536]{0:T(1024)S(1)} %copy-done.24), kind=kOutput, calls=%fused_computation.170 | convolution fusion | flops 2420637696 | bytes 11016192 | tf_op jit(solution)/shard_map/dot_general | solution.py:32
  93.9 4.1 %collective-permute-start.2 = (bf16[256,512]{1,0:T(8,128)(2,1)S(1)}, bf16[256,512]{1,0:T(8,128)(2,1)S(1)}, u32[]{:S(2)}, u32[]{:S(2)}) collective-permute-start(bf16[256,512]{1,0:T(8,128)(2,1)S(1)} %get-tuple-element.3), channel_id=1, source_target_pairs={{0,1},{1,2},{2,3},{3,4},{4,5},{5,6},{6,7},{7,8},{8,9},{9,10},{10,1... | collective-permute-start | bytes 786440 | tf_op jit(solution)/shard_map/ppermute | solution.py:12
  98.1 2.2 %collective-permute-start.3 = (bf16[256,512]{1,0:T(8,128)(2,1)S(1)}, bf16[256,512]{1,0:T(8,128)(2,1)S(1)}, u32[]{:S(2)}, u32[]{:S(2)}) collective-permute-start(bf16[256,512]{1,0:T(8,128)(2,1)S(1)} %get-tuple-element.4), channel_id=1, source_target_pairs={{1,0},{2,1},{3,2},{4,3},{5,4},{6,5},{7,6},{8,7},{9,8},{10,9},{11,1... | collective-permute-start | bytes 786440 | tf_op jit(solution)/shard_map/ppermute | solution.py:15
  100.3 3.4 %fusion.61 = bf16[256,512]{1,0:T(8,128)(2,1)} fusion(bf16[512,512]{1,0:T(8,128)(2,1)S(1)} %copy-done.6, f32[256,512]{1,0:T(8,128)S(1)} %fusion.36, bf16[256,512]{1,0:T(8,128)(2,1)S(1)} %fusion.60, s32[1536]{0:T(1024)S(1)} %copy-done.14, f32[1536,512]{1,0:T(8,128)} %fusion.10), kind=kOutput, calls=%fused_computation.87 | convolution fusion | flops 538836992 | bytes 4724736 | tf_op jit(solution)/shard_map/transpose(jvp())/dot_general | solution.py:91
  103.7 3.9 %collective-permute-done.3 = bf16[256,512]{1,0:T(8,128)(2,1)S(1)} collective-permute-done((bf16[256,512]{1,0:T(8,128)(2,1)S(1)}, bf16[256,512]{1,0:T(8,128)(2,1)S(1)}, u32[]{:S(2)}, u32[]{:S(2)}) %collective-permute-start.3) | collective-permute-done | bytes 262176 | tf_op jit(solution)/shard_map/ppermute | solution.py:15
  107.7 0.8 fusion.25
  108.5 1.8 %fusion.20 = bf16[1024,512]{1,0:T(8,128)(2,1)} fusion(f32[1536,512]{1,0:T(8,128)S(1)} %copy-done.9, f32[1024,512]{1,0:T(8,128)S(1)} %fusion.25, s32[512]{0:T(512)S(1)} %copy-done.20, f32[256,512]{1,0:T(8,128)S(1)} %get-tuple-element.6, f32[256,512]{1,0:T(8,128)S(1)} %get-tuple-element.5), kind=kOutput, calls=%fused_computation.40 | convolution fusion | flops 540016640 | bytes 6293504 | tf_op jit(solution)/shard_map/dot_general | solution.py:32
  110.4 3.6 %fusion.50 = bf16[227,1024]{1,0:T(8,128)(2,1)} fusion(bf16[227,512]{1,0:T(8,128)(2,1)S(1)} %copy-done.12, f32[1024,512]{1,0:T(8,128)S(1)} %copy-done.8, bf16[1024,512]{1,0:T(8,128)(2,1)} %fusion.20, bf16[512,512]{1,0:T(8,128)(2,1)} %param.26), kind=kOutput, calls=%fused_computation.76 | convolution fusion | flops 780897280 | bytes 4367360 | tf_op jit(solution)/shard_map/transpose(jvp())/dot_general | solution.py:63
  (62 shorter events, 0.5 us)
Async XLA Ops:
  0.6 43.5 %copy-start = (bf16[512,512]{1,0:T(8,128)(2,1)S(1)}, bf16[512,512]{1,0:T(8,128)(2,1)}, u32[]{:S(2)}) copy-start(bf16[512,512]{1,0:T(8,128)(2,1)} %param.31) | copy-start | bytes 1572868
  3.0 2.2 %copy-start.7 = (f32[1024,512]{1,0:T(8,128)}, f32[1024,512]{1,0:T(8,128)S(1)}, u32[]{:S(2)}) copy-start(f32[1024,512]{1,0:T(8,128)S(1)} %fusion.142) | copy-start | bytes 6291460
  5.2 4.6 %copy-start.25 = (bf16[1024,512]{1,0:T(8,128)(2,1)}, bf16[1024,512]{1,0:T(8,128)(2,1)S(1)}, u32[]{:S(2)}) copy-start(bf16[1024,512]{1,0:T(8,128)(2,1)S(1)} %convolution_convert_fusion.3) | copy-start | bytes 3145732
  5.2 6.5 %copy-start.21 = (s32[32,2]{0,1:T(2,128)S(1)}, s32[32,2]{0,1:T(2,128)}, u32[]{:S(2)}) copy-start(s32[32,2]{0,1:T(2,128)} %param.22) | copy-start | bytes 772
  5.2 6.7 %copy-start.6 = (bf16[512,512]{1,0:T(8,128)(2,1)S(1)}, bf16[512,512]{1,0:T(8,128)(2,1)}, u32[]{:S(2)}) copy-start(bf16[512,512]{1,0:T(8,128)(2,1)} %param.27) | copy-start | bytes 1572868
  5.2 6.7 %copy-start.10 = (bf16[256,512]{1,0:T(8,128)(2,1)S(1)}, bf16[256,512]{1,0:T(8,128)(2,1)}, u32[]{:S(2)}) copy-start(bf16[256,512]{1,0:T(8,128)(2,1)} %param.17) | copy-start | bytes 786436
  5.2 7.0 %copy-start.14 = (s32[1536]{0:T(1024)S(1)}, s32[1536]{0:T(1024)}, u32[]{:S(2)}) copy-start(s32[1536]{0:T(1024)} %param.21) | copy-start | bytes 18436
  5.2 7.6 %copy-start.19 = (s32[512]{0:T(512)}, s32[512]{0:T(512)S(1)}, u32[]{:S(2)}) copy-start(s32[512]{0:T(512)S(1)} %pad_add_fusion) | copy-start | bytes 6148
  6.0 7.5 %collective-permute-start = (bf16[256,512]{1,0:T(8,128)(2,1)S(1)}, bf16[256,512]{1,0:T(8,128)(2,1)S(1)}, u32[]{:S(2)}, u32[]{:S(2)}) collective-permute-start(bf16[256,512]{1,0:T(8,128)(2,1)S(1)} %get-tuple-element.7), channel_id=1, source_target_pairs={{0,1},{1,2},{2,3},{3,4},{4,5},{5,6},{6,7},{7,8},{8,9},{9,10},{10,1... | collective-permute-start | bytes 786440 | tf_op jit(solution)/shard_map/ppermute | solution.py:12
  9.7 9.5 %collective-permute-start.1 = (bf16[256,512]{1,0:T(8,128)(2,1)S(1)}, bf16[256,512]{1,0:T(8,128)(2,1)S(1)}, u32[]{:S(2)}, u32[]{:S(2)}) collective-permute-start(bf16[256,512]{1,0:T(8,128)(2,1)S(1)} %get-tuple-element.8), channel_id=1, source_target_pairs={{1,0},{2,1},{3,2},{4,3},{5,4},{6,5},{7,6},{8,7},{9,8},{10,9},{11,1... | collective-permute-start | bytes 786440 | tf_op jit(solution)/shard_map/ppermute | solution.py:15
  11.9 16.3 %copy-start.17 = (s32[64]{0:T(128)}, s32[64]{0:T(128)S(1)}, u32[]{:S(2)}) copy-start(s32[64]{0:T(128)S(1)} %eq.95) | copy-start | bytes 772
  12.8 6.4 %copy-start.23 = (s32[1536]{0:T(1024)S(1)}, s32[1536]{0:T(1024)}, u32[]{:S(2)}) copy-start(s32[1536]{0:T(1024)} %param.20) | copy-start | bytes 18436
  12.9 6.4 %copy-start.26 = (bf16[1024,512]{1,0:T(8,128)(2,1)S(1)}, bf16[1024,512]{1,0:T(8,128)(2,1)}, u32[]{:S(2)}) copy-start(bf16[1024,512]{1,0:T(8,128)(2,1)} %copy-done.25) | copy-start | bytes 3145732
  13.5 10.2 %copy-start.22 = (bf16[512,512]{1,0:T(8,128)(2,1)S(1)}, bf16[512,512]{1,0:T(8,128)(2,1)}, u32[]{:S(2)}) copy-start(bf16[512,512]{1,0:T(8,128)(2,1)} %param.28) | copy-start | bytes 1572868
  23.7 4.1 %copy-start.5 = (bf16[512,512]{1,0:T(8,128)(2,1)S(1)}, bf16[512,512]{1,0:T(8,128)(2,1)}, u32[]{:S(2)}) copy-start(bf16[512,512]{1,0:T(8,128)(2,1)} %param.29) | copy-start | bytes 1572868
  23.7 10.2 %copy-start.4 = (bf16[512,512]{1,0:T(8,128)(2,1)S(1)}, bf16[512,512]{1,0:T(8,128)(2,1)}, u32[]{:S(2)}) copy-start(bf16[512,512]{1,0:T(8,128)(2,1)} %param.30) | copy-start | bytes 1572868
  23.7 10.5 %copy-start.15 = (s32[2048]{0:T(1024)S(1)}, s32[2048]{0:T(1024)}, u32[]{:S(2)}) copy-start(s32[2048]{0:T(1024)} %param.24) | copy-start | bytes 24580
  29.0 10.2 %copy-start.13 = (s32[2048]{0:T(1024)S(1)}, s32[2048]{0:T(1024)}, u32[]{:S(2)}) copy-start(s32[2048]{0:T(1024)} %param.23) | copy-start | bytes 24580
  29.0 10.1 %all-to-all-start = ((bf16[32,2,512]{2,1,0:T(2,128)(2,1)}), bf16[32,2,512]{2,1,0:T(2,128)(2,1)S(1)}, u32[]{:S(2)}, u32[]{:S(2)}) async-start(bf16[32,2,512]{2,1,0:T(2,128)(2,1)} %reshape.26), calls=%async_computation | async-start | bytes 131072 | tf_op jit(solution)/shard_map/all_to_all | solution.py:125
  39.2 2.2 %copy-start.2 = (f32[2048,512]{1,0:T(8,128)S(1)}, f32[2048,512]{1,0:T(8,128)}, u32[]{:S(2)}) copy-start(f32[2048,512]{1,0:T(8,128)} %fusion.24) | copy-start | bytes 12582916
  41.4 2.8 %copy-start.16 = (s32[2048]{0:T(1024)S(1)}, s32[2048]{0:T(1024)}, u32[]{:S(2)}) copy-start(s32[2048]{0:T(1024)} %param.24) | copy-start | bytes 24580
  44.2 4.7 %copy-start.11 = (bf16[256,512]{1,0:T(8,128)(2,1)S(1)}, bf16[256,512]{1,0:T(8,128)(2,1)}, u32[]{:S(2)}) copy-start(bf16[256,512]{1,0:T(8,128)(2,1)} %param.18) | copy-start | bytes 786436
  55.2 5.1 %copy-start.1 = (f32[2048,512]{1,0:T(8,128)S(1)}, f32[2048,512]{1,0:T(8,128)}, u32[]{:S(2)}) copy-start(f32[2048,512]{1,0:T(8,128)} %fusion.6) | copy-start | bytes 12582916
  63.9 11.6 %copy-start.18 = (s32[64]{0:T(128)S(1)}, s32[64]{0:T(128)}, u32[]{:S(2)}) copy-start(s32[64]{0:T(128)} %copy-done.17) | copy-start | bytes 772
  63.9 10.8 %all-to-all-start.1 = ((bf16[32,2,512]{2,1,0:T(2,128)(2,1)}), bf16[32,2,512]{2,1,0:T(2,128)(2,1)}, u32[]{:S(2)}, u32[]{:S(2)}) async-start(bf16[32,2,512]{2,1,0:T(2,128)(2,1)} %convert_element_type.215), calls=%async_computation.1 | async-start | bytes 131072 | tf_op jit(solution)/shard_map/all_to_all | solution.py:152
  82.1 3.7 %copy-start.3 = (f32[1536,512]{1,0:T(8,128)S(1)}, f32[1536,512]{1,0:T(8,128)}, u32[]{:S(2)}) copy-start(f32[1536,512]{1,0:T(8,128)} %fusion.10) | copy-start | bytes 9437188
  82.2 3.7 %copy-start.24 = (s32[1536]{0:T(1024)S(1)}, s32[1536]{0:T(1024)}, u32[]{:S(2)}) copy-start(s32[1536]{0:T(1024)} %param.20) | copy-start | bytes 18436
  93.9 9.7 %collective-permute-start.2 = (bf16[256,512]{1,0:T(8,128)(2,1)S(1)}, bf16[256,512]{1,0:T(8,128)(2,1)S(1)}, u32[]{:S(2)}, u32[]{:S(2)}) collective-permute-start(bf16[256,512]{1,0:T(8,128)(2,1)S(1)} %get-tuple-element.3), channel_id=1, source_target_pairs={{0,1},{1,2},{2,3},{3,4},{4,5},{5,6},{6,7},{7,8},{8,9},{9,10},{10,1... | collective-permute-start | bytes 786440 | tf_op jit(solution)/shard_map/ppermute | solution.py:12
  98.1 9.6 %copy-start.20 = (s32[512]{0:T(512)S(1)}, s32[512]{0:T(512)}, u32[]{:S(2)}) copy-start(s32[512]{0:T(512)} %copy-done.19) | copy-start | bytes 6148
  98.1 9.5 %collective-permute-start.3 = (bf16[256,512]{1,0:T(8,128)(2,1)S(1)}, bf16[256,512]{1,0:T(8,128)(2,1)S(1)}, u32[]{:S(2)}, u32[]{:S(2)}) collective-permute-start(bf16[256,512]{1,0:T(8,128)(2,1)S(1)} %get-tuple-element.4), channel_id=1, source_target_pairs={{1,0},{2,1},{3,2},{4,3},{5,4},{6,5},{7,6},{8,7},{9,8},{10,9},{11,1... | collective-permute-start | bytes 786440 | tf_op jit(solution)/shard_map/ppermute | solution.py:15
  103.7 4.8 %copy-start.9 = (f32[1536,512]{1,0:T(8,128)S(1)}, f32[1536,512]{1,0:T(8,128)}, u32[]{:S(2)}) copy-start(f32[1536,512]{1,0:T(8,128)} %get-tuple-element.16) | copy-start | bytes 9437188
  108.5 1.9 %copy-start.8 = (f32[1024,512]{1,0:T(8,128)S(1)}, f32[1024,512]{1,0:T(8,128)}, u32[]{:S(2)}) copy-start(f32[1024,512]{1,0:T(8,128)} %copy-done.7) | copy-start | bytes 6291460
  108.5 1.9 %copy-start.12 = (bf16[227,512]{1,0:T(8,128)(2,1)S(1)}, bf16[227,512]{1,0:T(8,128)(2,1)}, u32[]{:S(2)}) copy-start(bf16[227,512]{1,0:T(8,128)(2,1)} %param.25) | copy-start | bytes 697348
where the time goes:
time: 115 us; the launch traced here: 114 us
  matrix products  72.2 us (63%)
  starting transfers between devices  22 us (19%)
  waiting for transfers between devices  14 us (12%)
  local copies, waits for them, and re-layouts  4.46 us (4%)
    dot_general x8, matrix products, carry_rows(): lax.dot_general(selector, low, dims, preferred_element_type=jnp.float32)  17.8 us
    dot_general x6, matrix products, carry_rows(): lax.dot_general(selector, high, dims, preferred_element_type=jnp.float32)  11.9 us
    ppermute x2, waiting for transfers between devices, padded(): lax.ppermute(lax.slice_in_dim(block, 0, width, axis=dim), axis, backward)  9.6 us
    ppermute x2, starting transfers between devices, padded(): lax.ppermute(lax.slice_in_dim(block, block.shape[dim] - width, None, axis...  7.8 us
    dot_general x1, matrix products, processor(): summed = jnp.dot(proc_onehot, message, preferred_element_type=jnp.float32)  6.27 us
    dot_general x1, matrix products, encoder(): summed = jnp.dot(enc_onehot, message, preferred_element_type=jnp.float32)  5.56 us
    all_to_all x1, starting transfers between devices, local(): lax.all_to_all(grad_received.astype(jnp.bfloat16), 'band', split_axis=0,...  5.31 us
    dot_general x2, matrix products, embedding(): lax.dot_general(grid_values, w_embed, (((0,), (0,)), ((), ())), preferred...  5.14 us
  transfers between devices with their start and end apart: 6, of which 4 were waited for; matrix products, arithmetic and copies ran while one was open for 10% of the time, Pallas kernels for 0%

commit v1 on v0

--- a/solution.py
+++ b/solution.py
@@ -26,11 +26,8 @@
 
 
 def carry_rows(selector, values, axis):
-    high = values.astype(jnp.bfloat16)
-    low = (values - high.astype(jnp.float32)).astype(jnp.bfloat16)
     dims = (((axis,), (0,)), ((), ()))
-    first = lax.dot_general(selector, high, dims, preferred_element_type=jnp.float32)
-    return first + lax.dot_general(selector, low, dims, preferred_element_type=jnp.float32)
+    return lax.dot_general(selector, values.astype(jnp.bfloat16), dims, preferred_element_type=jnp.float32)
 
 
 def local(

time: 115 us -> 113 us (0.983)
  blocking collectives: 0 us -> 10 us
  starting transfers between devices: 22 us -> 16.9 us
  matrix products: 72.2 us -> 68 us
  waiting for transfers between devices: 14 us -> 10.6 us
  local copies, waits for them, and re-layouts: 4.46 us -> 5.65 us
    all_to_all x0 -> x1, blocking collectives: none -> 10 us  [local(): lax.all_to_all(outbound, 'band', split_axis=0, concat_axis=0, tiled=True)]
    dot_general x14 -> x6, matrix products: 29.7 us -> 23.1 us  [carry_rows(): lax.dot_general(selector, values.astype(jnp.bfloat16), dims, preferred_el...]
    all_to_all x1 -> x0, starting transfers between devices: 4.83 us -> none  [local(): lax.all_to_all(outbound, 'band', split_axis=0, concat_axis=0, tiled=True)]
    dot_general x1, matrix products: 4.47 us -> 6.76 us  [local(): jnp.dot(source_select, grid_table, preferred_element_type=jnp.float32)]
    all_to_all x1 -> x0, waiting for transfers between devices: 2.23 us -> none  [local(): lax.all_to_all(outbound, 'band', split_axis=0, concat_axis=0, tiled=True)]
    dot_general x2, matrix products: 0.63 us -> 2.62 us  [projection(): jnp.dot(latent_values.astype(jnp.bfloat16), w_sender, preferred_element_t...]
    dot_general x1, matrix products: 1.31 us -> 2.87 us  [local(): jnp.dot(proc_select, mesh_table, preferred_element_type=jnp.float32)]
    slice x2, local copies, waits for them, and re-layouts: 0.07 us -> 1.55 us  [padded(): lax.slice_in_dim(block, block.shape[dim] - width, None, axis=dim)]
  transfers between devices with their start and end apart: 6 -> 5, of which waited for: 4 -> 3; matrix products, arithmetic and copies ran while one was open for 10% -> 9% of each run, Pallas kernels for 0% -> 0%
where the time goes in v1:
time: 113 us; the launch traced here: 112 us
  matrix products  68 us (60%)
  starting transfers between devices  16.9 us (15%)
  waiting for transfers between devices  10.6 us (9%)
  blocking collectives  10 us (9%)
  local copies, waits for them, and re-layouts  5.65 us (5%)
    dot_general x6, matrix products, carry_rows(): lax.dot_general(selector, values.astype(jnp.bfloat16), dims, preferred_el...  23.1 us
    all_to_all x1, blocking collectives, local(): lax.all_to_all(outbound, 'band', split_axis=0, concat_axis=0, tiled=True)  10 us
    ppermute x2, waiting for transfers between devices, padded(): lax.ppermute(lax.slice_in_dim(block, 0, width, axis=dim), axis, backward)  8.69 us
    ppermute x2, starting transfers between devices, padded(): lax.ppermute(lax.slice_in_dim(block, block.shape[dim] - width, None, axis...  8.2 us
    dot_general x1, matrix products, local(): jnp.dot(source_select, grid_table, preferred_element_type=jnp.float32)  6.76 us
    dot_general x1, matrix products, processor(): summed = jnp.dot(proc_onehot, message, preferred_element_type=jnp.float32)  5.37 us
    dot_general x1, matrix products, encoder(): summed = jnp.dot(enc_onehot, message, preferred_element_type=jnp.float32)  5.18 us
    dot_general x2, matrix products, embedding(): lax.dot_general(grid_values, w_embed, (((0,), (0,)), ((), ())), preferred...  5 us
  transfers between devices with their start and end apart: 5, of which 3 were waited for; matrix products, arithmetic and copies ran while one was open for 9% of the time, Pallas kernels for 0%

profile of v1, /device:TPU:7, one launch (start us, length us, event | category | flops | bytes accessed | tf_op | source)
XLA Modules:
  0.0 112.0 jit_solution(176650492474925350)
XLA Ops:
  0.6 0.0 copy-start
  0.6 0.0 copy-start.16
  0.7 0.8 fusion.111
  1.4 1.6 %fusion.113 = f32[1024,512]{1,0:T(8,128)S(1)} fusion(bf16[227,1024]{1,0:T(8,128)(2,1)} %param.16, bf16[227,512]{1,0:T(8,128)(2,1)} %param.25), kind=kOutput, calls=%fused_computation.136 | convolution fusion | flops 238026752 | bytes 2794496 | tf_op jit(solution)/shard_map/jvp()/dot_general | solution.py:60
  3.0 0.7 convolution_convert_fusion.3
  3.8 0.6 copy-done.13
  4.4 0.7 fusion.33
  5.1 0.7 fusion.110
  5.9 3.8 %collective-permute-start = (bf16[256,512]{1,0:T(8,128)(2,1)}, bf16[256,512]{1,0:T(8,128)(2,1)}, u32[]{:S(2)}, u32[]{:S(2)}) collective-permute-start(bf16[256,512]{1,0:T(8,128)(2,1)} %get-tuple-element.5), channel_id=1, source_target_pairs={{0,1},{1,2},{2,3},{3,4},{4,5},{5,6},{6,7},{7,8},{8,9},{9,10},{10,1... | collective-permute-start | bytes 786440 | tf_op jit(solution)/shard_map/ppermute | solution.py:12
  9.7 1.9 %collective-permute-start.1 = (bf16[256,512]{1,0:T(8,128)(2,1)S(1)}, bf16[256,512]{1,0:T(8,128)(2,1)}, u32[]{:S(2)}, u32[]{:S(2)}) collective-permute-start(bf16[256,512]{1,0:T(8,128)(2,1)S(1)} %get-tuple-element.6), channel_id=1, source_target_pairs={{1,0},{2,1},{3,2},{4,3},{5,4},{6,5},{7,6},{8,7},{9,8},{10,9},{11,1... | collective-permute-start | bytes 786440 | tf_op jit(solution)/shard_map/ppermute | solution.py:15
  11.6 0.0 copy-done.15
  11.6 0.1 copy.20
  11.7 0.1 eq.95
  11.8 0.0 copy-start.11
  11.9 3.5 %fusion.32 = f32[1536,512]{1,0:T(8,128)} fusion(bf16[256,512]{1,0:T(8,128)(2,1)} %param.17, bf16[512,512]{1,0:T(8,128)(2,1)S(1)} %copy-done.4, s32[1536]{0:T(1024)S(1)} %copy-done.9), kind=kOutput, calls=%fused_computation.54 | convolution fusion | flops 537395200 | bytes 3938304 | tf_op jit(solution)/shard_map/dot_general | solution.py:30
  15.3 0.0 collective-permute-done
  15.3 4.0 %collective-permute-done.1 = bf16[256,512]{1,0:T(8,128)(2,1)} collective-permute-done((bf16[256,512]{1,0:T(8,128)(2,1)S(1)}, bf16[256,512]{1,0:T(8,128)(2,1)}, u32[]{:S(2)}, u32[]{:S(2)}) %collective-permute-start.1) | collective-permute-done | bytes 262176 | tf_op jit(solution)/shard_map/ppermute | solution.py:15
  19.3 6.8 %fusion.7 = f32[1536,512]{1,0:T(8,128)} fusion(f32[1536,512]{1,0:T(8,128)} %fusion.32, s32[1536]{0:T(1024)S(1)} %copy-done.18, bf16[256,512]{1,0:T(8,128)(2,1)} %collective-permute-done.1, bf16[256,512]{1,0:T(8,128)(2,1)} %collective-permute-done, bf16[1024,512]{1,0:T(8,128)(2,1)} %copy-done.20), kind=kOutput, calls=%fused_computation.17 | convolution fusion | flops 2423783424 | bytes 7870464 | tf_op jit(solution)/shard_map/dot_general | solution.py:78
  26.1 4.3 %add_convert_fusion.1 = (bf16[256,512]{1,0:T(8,128)(2,1)}, f32[256,512]{1,0:T(8,128)}) fusion(bf16[256,512]{1,0:T(8,128)(2,1)S(1)} %copy-done.6, bf16[512,512]{1,0:T(8,128)(2,1)} %param.28, f32[1536,512]{1,0:T(8,128)} %fusion.7, s32[1536]{0:T(1024)S(1)} %copy-done.9), kind=kOutput, calls=%fused_computation.111 | convolution fusion | flops 542244864 | bytes 4724736 | tf_op jit(solution)/shard_map/jvp()/dot_general | solution.py:101
  30.4 1.2 %convolution_convert_fusion.6 = bf16[256,512]{1,0:T(8,128)(2,1)S(1)} fusion(bf16[256,512]{1,0:T(8,128)(2,1)} %get-tuple-element.9, bf16[512,512]{1,0:T(8,128)(2,1)S(1)} %copy-done.1), kind=kOutput, calls=%fused_computation.75 | convolution fusion | flops 134348800 | bytes 1048576 | tf_op jit(solution)/shard_map/jvp()/dot_general | solution.py:109
  31.6 0.2 convolution_convert_fusion.10
  31.9 10.0 %all_to_all.10 = bf16[32,2,512]{2,1,0:T(2,128)(2,1)} all-to-all(bf16[32,2,512]{2,1,0:T(2,128)(2,1)S(1)} %reshape.22), channel_id=1, replica_groups=mesh['band'=32] {'band'}, dimensions={0} | all-to-all | bytes 131072 | tf_op jit(solution)/shard_map/all_to_all | solution.py:122
  41.9 0.9 reshape.23
  42.8 0.0 copy-start.10
  42.8 2.9 %fusion.12 = f32[2048,512]{1,0:T(8,128)} fusion(s32[2048]{0:T(1024)S(1)} %copy-done.8, bf16[64,512]{1,0:T(8,128)(2,1)S(1)} %reshape.23, bf16[256,512]{1,0:T(8,128)(2,1)S(1)} %convolution_convert_fusion.6), kind=kOutput, calls=%fused_computation.24 | convolution fusion | flops 672399360 | bytes 4530176 | tf_op jit(solution)/shard_map/dot_general | solution.py:126
  45.7 5.4 %convolution_add_fusion = f32[2048,512]{1,0:T(8,128)} fusion(f32[2048,512]{1,0:T(8,128)} %fusion.12, bf16[256,512]{1,0:T(8,128)(2,1)} %get-tuple-element.9, bf16[512,512]{1,0:T(8,128)(2,1)} %param.30, s32[2048]{0:T(1024)S(1)} %copy-done.10), kind=kOutput, calls=%fused_computation.16 | convolution fusion | flops 672792576 | bytes 9183232 | tf_op jit(solution)/shard_map/dot_general | solution.py:30
  51.1 4.8 %add_convert_fusion = (bf16[256,512]{1,0:T(8,128)(2,1)}, f32[256,512]{1,0:T(8,128)}) fusion(bf16[256,512]{1,0:T(8,128)(2,1)S(1)} %copy-done.2, bf16[512,512]{1,0:T(8,128)(2,1)S(1)} %copy-done, f32[2048,512]{1,0:T(8,128)} %convolution_add_fusion, s32[2048]{0:T(1024)S(1)} %copy-done.10), kind=kOutput, calls=%fused_computation.109 | convolution fusion | flops 677904384 | bytes 5775360 | tf_op jit(solution)/shard_map/jvp()/dot_general | solution.py:140
  55.9 5.4 %fusion.5 = bf16[2048,512]{1,0:T(8,128)(2,1)} fusion(f32[2048,512]{1,0:T(8,128)} %convolution_add_fusion, bf16[512,512]{1,0:T(8,128)(2,1)S(1)} %copy-done, s32[2048]{0:T(1024)S(1)} %copy-done.10, bf16[256,512]{1,0:T(8,128)(2,1)} %param.18, f32[256,512]{1,0:T(8,128)} %get-tuple-element.12), kind=kOutput, calls=%fused_computation.10 | convolution fusion | flops 685637632 | bytes 7610368 | tf_op jit(solution)/shard_map/transpose(jvp())/dot_general | solution.py:138
  61.2 3.0 %fusion.11 = f32[320,512]{1,0:T(8,128)S(1)} fusion(bf16[2048,512]{1,0:T(8,128)(2,1)} %fusion.5, s32[2048]{0:T(1024)S(1)} %copy-done.8), kind=kOutput, calls=%fused_computation.23 | convolution fusion | flops 671744000 | bytes 2760704 | tf_op jit(solution)/shard_map/dot_general | solution.py:30
  64.3 0.8 copy-done.3
  65.1 0.7 convert_element_type.170
  65.8 4.6 %all-to-all-start.1 = ((bf16[32,2,512]{2,1,0:T(2,128)(2,1)}), bf16[32,2,512]{2,1,0:T(2,128)(2,1)S(1)}, u32[]{:S(2)}, u32[]{:S(2)}) async-start(bf16[32,2,512]{2,1,0:T(2,128)(2,1)} %convert_element_type.170), calls=%async_computation.1 | async-start | bytes 131072 | tf_op jit(solution)/shard_map/all_to_all | solution.py:149
  70.4 0.0 copy-start.12
  70.4 3.5 %fusion.54 = f32[256,512]{1,0:T(8,128)} fusion(bf16[512,512]{1,0:T(8,128)(2,1)} %param.30, bf16[2048,512]{1,0:T(8,128)(2,1)} %fusion.5, s32[2048]{0:T(1024)S(1)} %copy-done.10, bf16[256,512]{1,0:T(8,128)(2,1)} %param.18), kind=kOutput, calls=%fused_computation.79 | convolution fusion | flops 672137216 | bytes 3416064 | tf_op jit(solution)/shard_map/transpose(jvp())/dot_general | solution.py:129
  73.9 1.9 %all-to-all-done.1 = bf16[32,2,512]{2,1,0:T(2,128)(2,1)S(1)} async-done(((bf16[32,2,512]{2,1,0:T(2,128)(2,1)}), bf16[32,2,512]{2,1,0:T(2,128)(2,1)S(1)}, u32[]{:S(2)}, u32[]{:S(2)}) %all-to-all-start.1) | async-done | bytes 65568 | tf_op jit(solution)/shard_map/all_to_all | solution.py:149
  75.9 1.4 %fusion.43 = bf16[256,512]{1,0:T(8,128)(2,1)S(1)} fusion(bf16[64,512]{1,0:T(8,128)(2,1)S(1)} %convert_element_type.171, f32[320,512]{1,0:T(8,128)} %copy-done.3, s32[64]{0:T(128)S(1)} %copy-done.12), kind=kOutput, calls=%fused_computation.64 | convolution fusion | flops 17055744 | bytes 852224 | tf_op jit(solution)/shard_map/dot_general | solution.py:30
  77.2 1.4 %fusion.51 = bf16[256,512]{1,0:T(8,128)(2,1)S(1)} fusion(f32[256,512]{1,0:T(8,128)} %fusion.54, bf16[256,512]{1,0:T(8,128)(2,1)S(1)} %fusion.43, bf16[512,512]{1,0:T(8,128)(2,1)S(1)} %copy-done.1), kind=kOutput, calls=%fused_computation.73 | convolution fusion | flops 134742016 | bytes 1572864 | tf_op jit(solution)/shard_map/transpose(jvp())/dot_general | solution.py:109
  78.6 0.0 copy-start.19
  78.6 5.2 %fusion.9 = bf16[1536,512]{1,0:T(8,128)(2,1)} fusion(f32[1536,512]{1,0:T(8,128)} %fusion.7, bf16[512,512]{1,0:T(8,128)(2,1)} %param.28, s32[1536]{0:T(1024)S(1)} %copy-done.9, bf16[256,512]{1,0:T(8,128)(2,1)S(1)} %fusion.51, f32[256,512]{1,0:T(8,128)} %get-tuple-element.10), kind=kOutput, calls=%fused_computation.19 | convolution fusion | flops 548143104 | bytes 6035456 | tf_op jit(solution)/shard_map/transpose(jvp())/dot_general | solution.py:97
  83.8 6.2 %fusion.112 = (bf16[1536,512]{1,0:T(8,128)(2,1)S(1)}, f32[1536,512]{1,0:T(8,128)}) fusion(bf16[1536,512]{1,0:T(8,128)(2,1)} %fusion.9, s32[1536]{0:T(1024)S(1)} %copy-done.19), kind=kOutput, calls=%fused_computation.135 | convolution fusion | flops 2419064832 | bytes 6297600 | tf_op jit(solution)/shard_map/dot_general | solution.py:30
  90.0 0.8 fusion.109
  90.8 4.4 %collective-permute-start.2 = (bf16[256,512]{1,0:T(8,128)(2,1)}, bf16[256,512]{1,0:T(8,128)(2,1)}, u32[]{:S(2)}, u32[]{:S(2)}) collective-permute-start(bf16[256,512]{1,0:T(8,128)(2,1)} %get-tuple-element.3), channel_id=1, source_target_pairs={{0,1},{1,2},{2,3},{3,4},{4,5},{5,6},{6,7},{7,8},{8,9},{9,10},{10,1... | collective-permute-start | bytes 786440 | tf_op jit(solution)/shard_map/ppermute | solution.py:12
  95.2 2.1 %collective-permute-start.3 = (bf16[256,512]{1,0:T(8,128)(2,1)}, bf16[256,512]{1,0:T(8,128)(2,1)}, u32[]{:S(2)}, u32[]{:S(2)}) collective-permute-start(bf16[256,512]{1,0:T(8,128)(2,1)} %get-tuple-element.4), channel_id=1, source_target_pairs={{1,0},{2,1},{3,2},{4,3},{5,4},{6,5},{7,6},{8,7},{9,8},{10,9},{11,1... | collective-permute-start | bytes 786440 | tf_op jit(solution)/shard_map/ppermute | solution.py:15
  97.4 2.9 %fusion.47 = bf16[256,512]{1,0:T(8,128)(2,1)} fusion(bf16[512,512]{1,0:T(8,128)(2,1)S(1)} %copy-done.5, bf16[1536,512]{1,0:T(8,128)(2,1)} %fusion.9, bf16[256,512]{1,0:T(8,128)(2,1)S(1)} %fusion.51, s32[1536]{0:T(1024)S(1)} %copy-done.9), kind=kOutput, calls=%fused_computation.68 | convolution fusion | flops 537919488 | bytes 2627584 | tf_op jit(solution)/shard_map/transpose(jvp())/dot_general | solution.py:88
  100.3 0.0 collective-permute-done.2
  100.3 4.7 %collective-permute-done.3 = bf16[256,512]{1,0:T(8,128)(2,1)} collective-permute-done((bf16[256,512]{1,0:T(8,128)(2,1)}, bf16[256,512]{1,0:T(8,128)(2,1)}, u32[]{:S(2)}, u32[]{:S(2)}) %collective-permute-start.3) | collective-permute-done | bytes 262176 | tf_op jit(solution)/shard_map/ppermute | solution.py:15
  105.0 3.6 %fusion.18 = bf16[1024,512]{1,0:T(8,128)(2,1)} fusion(f32[1536,512]{1,0:T(8,128)} %get-tuple-element.14, s32[512]{0:T(512)S(1)} %copy-done.14, bf16[256,512]{1,0:T(8,128)(2,1)} %collective-permute-done.3, bf16[256,512]{1,0:T(8,128)(2,1)} %collective-permute-done.2), kind=kOutput, calls=%fused_computation.35 | convolution fusion | flops 539492352 | bytes 3672064 | tf_op jit(solution)/shard_map/dot_general | solution.py:30
  108.6 3.4 %fusion.39 = bf16[227,1024]{1,0:T(8,128)(2,1)} fusion(bf16[227,512]{1,0:T(8,128)(2,1)S(1)} %copy-done.7, f32[1024,512]{1,0:T(8,128)S(1)} %fusion.113, bf16[1024,512]{1,0:T(8,128)(2,1)} %fusion.18, bf16[512,512]{1,0:T(8,128)(2,1)S(1)} %copy-done.17), kind=kOutput, calls=%fused_computation.62 | convolution fusion | flops 780897280 | bytes 4367360 | tf_op jit(solution)/shard_map/transpose(jvp())/dot_general | solution.py:60
  (37 shorter events, 0.2 us)
Async XLA Ops:
  0.6 50.5 %copy-start = (bf16[512,512]{1,0:T(8,128)(2,1)S(1)}, bf16[512,512]{1,0:T(8,128)(2,1)}, u32[]{:S(2)}) copy-start(bf16[512,512]{1,0:T(8,128)(2,1)} %param.31) | copy-start | bytes 1572868
  0.6 2.4 %copy-start.16 = (bf16[512,512]{1,0:T(8,128)(2,1)S(1)}, bf16[512,512]{1,0:T(8,128)(2,1)}, u32[]{:S(2)}) copy-start(bf16[512,512]{1,0:T(8,128)(2,1)} %param.26) | copy-start | bytes 1572868
  3.8 5.9 %copy-start.20 = (bf16[1024,512]{1,0:T(8,128)(2,1)}, bf16[1024,512]{1,0:T(8,128)(2,1)S(1)}, u32[]{:S(2)}) copy-start(bf16[1024,512]{1,0:T(8,128)(2,1)S(1)} %convolution_convert_fusion.3) | copy-start | bytes 3145732
  3.8 0.6 copy-start.13
  4.4 7.2 %copy-start.15 = (s32[32,2]{0,1:T(2,128)S(1)}, s32[32,2]{0,1:T(2,128)}, u32[]{:S(2)}) copy-start(s32[32,2]{0,1:T(2,128)} %param.22) | copy-start | bytes 772
  4.4 7.4 %copy-start.4 = (bf16[512,512]{1,0:T(8,128)(2,1)S(1)}, bf16[512,512]{1,0:T(8,128)(2,1)}, u32[]{:S(2)}) copy-start(bf16[512,512]{1,0:T(8,128)(2,1)} %param.27) | copy-start | bytes 1572868
  4.4 7.5 %copy-start.9 = (s32[1536]{0:T(1024)S(1)}, s32[1536]{0:T(1024)}, u32[]{:S(2)}) copy-start(s32[1536]{0:T(1024)} %param.21) | copy-start | bytes 18436
  5.9 13.4 %copy-start.18 = (s32[1536]{0:T(1024)S(1)}, s32[1536]{0:T(1024)}, u32[]{:S(2)}) copy-start(s32[1536]{0:T(1024)} %param.20) | copy-start | bytes 18436
  5.9 9.5 %collective-permute-start = (bf16[256,512]{1,0:T(8,128)(2,1)}, bf16[256,512]{1,0:T(8,128)(2,1)}, u32[]{:S(2)}, u32[]{:S(2)}) collective-permute-start(bf16[256,512]{1,0:T(8,128)(2,1)} %get-tuple-element.5), channel_id=1, source_target_pairs={{0,1},{1,2},{2,3},{3,4},{4,5},{5,6},{6,7},{7,8},{8,9},{9,10},{10,1... | collective-permute-start | bytes 786440 | tf_op jit(solution)/shard_map/ppermute | solution.py:12
  9.7 9.6 %collective-permute-start.1 = (bf16[256,512]{1,0:T(8,128)(2,1)S(1)}, bf16[256,512]{1,0:T(8,128)(2,1)}, u32[]{:S(2)}, u32[]{:S(2)}) collective-permute-start(bf16[256,512]{1,0:T(8,128)(2,1)S(1)} %get-tuple-element.6), channel_id=1, source_target_pairs={{1,0},{2,1},{3,2},{4,3},{5,4},{6,5},{7,6},{8,7},{9,8},{10,9},{11,1... | collective-permute-start | bytes 786440 | tf_op jit(solution)/shard_map/ppermute | solution.py:15
  11.8 19.8 %copy-start.11 = (s32[64]{0:T(128)}, s32[64]{0:T(128)S(1)}, u32[]{:S(2)}) copy-start(s32[64]{0:T(128)S(1)} %eq.95) | copy-start | bytes 772
  19.3 6.8 %copy-start.6 = (bf16[256,512]{1,0:T(8,128)(2,1)S(1)}, bf16[256,512]{1,0:T(8,128)(2,1)}, u32[]{:S(2)}) copy-start(bf16[256,512]{1,0:T(8,128)(2,1)} %param.17) | copy-start | bytes 786436
  26.1 4.3 %copy-start.1 = (bf16[512,512]{1,0:T(8,128)(2,1)S(1)}, bf16[512,512]{1,0:T(8,128)(2,1)}, u32[]{:S(2)}) copy-start(bf16[512,512]{1,0:T(8,128)(2,1)} %param.29) | copy-start | bytes 1572868
  26.1 16.7 %copy-start.8 = (s32[2048]{0:T(1024)S(1)}, s32[2048]{0:T(1024)}, u32[]{:S(2)}) copy-start(s32[2048]{0:T(1024)} %param.23) | copy-start | bytes 24580
  42.8 2.9 %copy-start.10 = (s32[2048]{0:T(1024)S(1)}, s32[2048]{0:T(1024)}, u32[]{:S(2)}) copy-start(s32[2048]{0:T(1024)} %param.24) | copy-start | bytes 24580
  45.7 5.4 %copy-start.2 = (bf16[256,512]{1,0:T(8,128)(2,1)S(1)}, bf16[256,512]{1,0:T(8,128)(2,1)}, u32[]{:S(2)}) copy-start(bf16[256,512]{1,0:T(8,128)(2,1)} %get-tuple-element.9) | copy-start | bytes 786436
  64.3 0.8 copy-start.3
  65.8 10.0 %all-to-all-start.1 = ((bf16[32,2,512]{2,1,0:T(2,128)(2,1)}), bf16[32,2,512]{2,1,0:T(2,128)(2,1)S(1)}, u32[]{:S(2)}, u32[]{:S(2)}) async-start(bf16[32,2,512]{2,1,0:T(2,128)(2,1)} %convert_element_type.170), calls=%async_computation.1 | async-start | bytes 131072 | tf_op jit(solution)/shard_map/all_to_all | solution.py:149
  70.4 5.4 %copy-start.12 = (s32[64]{0:T(128)S(1)}, s32[64]{0:T(128)}, u32[]{:S(2)}) copy-start(s32[64]{0:T(128)} %copy-done.11) | copy-start | bytes 772
  78.6 5.2 %copy-start.19 = (s32[1536]{0:T(1024)S(1)}, s32[1536]{0:T(1024)}, u32[]{:S(2)}) copy-start(s32[1536]{0:T(1024)} %param.20) | copy-start | bytes 18436
  83.8 13.5 %copy-start.5 = (bf16[512,512]{1,0:T(8,128)(2,1)S(1)}, bf16[512,512]{1,0:T(8,128)(2,1)}, u32[]{:S(2)}) copy-start(bf16[512,512]{1,0:T(8,128)(2,1)} %param.27) | copy-start | bytes 1572868
  90.8 14.2 %copy-start.14 = (s32[512]{0:T(512)S(1)}, s32[512]{0:T(512)}, u32[]{:S(2)}) copy-start(s32[512]{0:T(512)} %copy-done.13) | copy-start | bytes 6148
  90.8 9.5 %collective-permute-start.2 = (bf16[256,512]{1,0:T(8,128)(2,1)}, bf16[256,512]{1,0:T(8,128)(2,1)}, u32[]{:S(2)}, u32[]{:S(2)}) collective-permute-start(bf16[256,512]{1,0:T(8,128)(2,1)} %get-tuple-element.3), channel_id=1, source_target_pairs={{0,1},{1,2},{2,3},{3,4},{4,5},{5,6},{6,7},{7,8},{8,9},{9,10},{10,1... | collective-permute-start | bytes 786440 | tf_op jit(solution)/shard_map/ppermute | solution.py:12
  95.2 9.8 %collective-permute-start.3 = (bf16[256,512]{1,0:T(8,128)(2,1)}, bf16[256,512]{1,0:T(8,128)(2,1)}, u32[]{:S(2)}, u32[]{:S(2)}) collective-permute-start(bf16[256,512]{1,0:T(8,128)(2,1)} %get-tuple-element.4), channel_id=1, source_target_pairs={{1,0},{2,1},{3,2},{4,3},{5,4},{6,5},{7,6},{8,7},{9,8},{10,9},{11,1... | collective-permute-start | bytes 786440 | tf_op jit(solution)/shard_map/ppermute | solution.py:15
  100.3 8.3 %copy-start.7 = (bf16[227,512]{1,0:T(8,128)(2,1)S(1)}, bf16[227,512]{1,0:T(8,128)(2,1)}, u32[]{:S(2)}) copy-start(bf16[227,512]{1,0:T(8,128)(2,1)} %param.25) | copy-start | bytes 697348
  100.3 8.3 %copy-start.17 = (bf16[512,512]{1,0:T(8,128)(2,1)S(1)}, bf16[512,512]{1,0:T(8,128)(2,1)}, u32[]{:S(2)}) copy-start(bf16[512,512]{1,0:T(8,128)(2,1)} %param.26) | copy-start | bytes 1572868

commit v2 on v1

v2 whole, which is shorter than its diff:
```python
import functools

import jax
import jax.numpy as jnp
from jax import lax
from jax.experimental import pallas as pl
from jax.experimental.pallas import tpu as pltpu
from jax.sharding import PartitionSpec as P

F32 = jnp.float32
BF16 = jnp.bfloat16
MESH = pl.DeviceIdType.MESH
LANES = 128
TILE = 512


def nn(left, right):
    return jnp.dot(left, right, preferred_element_type=F32)


def nt(left, right):
    return lax.dot_general(left, right, (((1,), (1,)), ((), ())), preferred_element_type=F32)


def tn(left, right):
    return lax.dot_general(left, right, (((0,), (0,)), ((), ())), preferred_element_type=F32)


def gate(values):
    sigmoid = 0.5 * jnp.tanh(0.5 * values) + 0.5
    out = values * sigmoid
    return out, sigmoid + out - out * sigmoid


def pick(column, base, width, shift=0):
    lane = lax.broadcasted_iota(jnp.int32, column.shape, 1)
    parts = [
        jnp.where(column == lax.shift_right_logical(lane + k, shift) + base, 1.0, 0.0).astype(BF16)
        for k in range(0, width, LANES)
    ]
    return jnp.concatenate(parts, axis=1)


def spread(index_ref, first, groups, base, rows, shift=0):
    row = lax.broadcasted_iota(jnp.int32, (rows, LANES), 0)
    row = lax.shift_right_logical(row, shift) + base
    parts = [
        jnp.where(index_ref[g : g + 1, :] == row, 1.0, 0.0).astype(BF16)
        for g in range(first, first + groups)
    ]
    return jnp.concatenate(parts, axis=1)


def block_rows(shape, blocks):
    return lax.broadcasted_iota(jnp.int32, shape, 0) & (blocks - 1)


def packed(full, blocks):
    which = block_rows((full.shape[0], LANES), blocks)
    out = full[:, :LANES]
    for c in range(1, blocks):
        out = jnp.where(which == c, full[:, c * LANES : (c + 1) * LANES], out)
    return out


def unpacked(part, blocks):
    which = block_rows(part.shape, blocks)
    return jnp.concatenate(
        [jnp.where(which == c, part, 0.0).astype(BF16) for c in range(blocks)], axis=1
    )


def kernel(
    n,
    at,
    enc_source_ref,
    enc_target_ref,
    proc_source_ref,
    proc_target_ref,
    lists_ref,
    mesh_lists_ref,
    grid_in,
    mesh_ref,
    cot_ref,
    embed_in,
    w_source,
    w_target,
    w_node,
    w_sender,
    w_receiver,
    w_update,
    out_ref,
    grad_grid_ref,
    grad_mesh_ref,
    index_ref,
    column,
    grid_ref,
    w_embed,
    list_hot,
    table,
    halo,
    halo_send,
    halo_recv,
    back,
    back_send,
    pre,
    edge,
    grad_part,
    slope_grid,
    slope_halo,
    slope_enc,
    slope_proc,
    pair,
    hot_halo,
    hot_enc,
    row_enc,
    row_halo,
    hot_far,
    hot_proc,
    row_proc,
    row_far,
    hot_lists,
    slab_send,
    slab_recv,
    turn_send,
    turn_recv,
    halo_sems,
    slab_sems,
):
    me = lax.axis_index("band")
    channels, grid_count = grid_in.shape
    nodes, width = mesh_ref.shape
    half = halo.shape[0] // 2
    enc = slope_enc.shape[0]
    proc = slope_proc.shape[0]
    slots = mesh_lists_ref.shape[0]
    blocks = width // LANES
    shift = blocks.bit_length() - 1
    per = slots * blocks
    slabs = n * per
    deep = grid_ref.shape[0]

    def exchange(source, target, k, kind):
        device = lax.rem(me + (n - 1 if k == 0 else 1), n)
        return pltpu.make_async_remote_copy(
            src_ref=source.at[pl.ds(k * half, half)],
            dst_ref=target.at[pl.ds((1 - k) * half, half)],
            send_sem=halo_sems.at[kind, 0, k],
            recv_sem=halo_sems.at[kind, 1, k],
            device_id=(device,),
            device_id_type=MESH,
        )

    def exchange_start(source, target, kind):
        @pl.when(me > 0)
        def _():
            exchange(source, target, 0, kind).start()

        @pl.when(me < n - 1)
        def _():
            exchange(source, target, 1, kind).start()

    def exchange_wait(source, target, kind):
        @pl.when(me < n - 1)
        def _():
            exchange(source, target, 0, kind).wait_recv()
            exchange(source, target, 1, kind).wait_send()

        @pl.when(me > 0)
        def _():
            exchange(source, target, 1, kind).wait_recv()
            exchange(source, target, 0, kind).wait_send()

    def scatter_start(source, target, kind):
        def send(k, carry):
            other = lax.rem(me + k, n)
            pltpu.make_async_remote_copy(
                src_ref=source.at[other],
                dst_ref=target.at[me],
                send_sem=slab_sems.at[kind, 0],
                recv_sem=slab_sems.at[kind, 1],
                device_id=(other,),
                device_id_type=MESH,
            ).start()
            return carry

        lax.fori_loop(1, n, send, 0)

    def scatter_wait(source, target, kind):
        whole_source = source.at[pl.ds(0, n - 1)]
        whole_target = target.at[pl.ds(0, n - 1)]
        pltpu.make_async_copy(whole_source, whole_target, slab_sems.at[kind, 0]).wait()
        pltpu.make_async_copy(whole_source, whole_target, slab_sems.at[kind, 1]).wait()

    @pl.when(me == 0)
    def _():
        halo_recv[pl.ds(0, half), :] = jnp.zeros((half, deep), BF16)
        back[pl.ds(0, half), :] = jnp.zeros((half, deep), BF16)

    @pl.when(me == n - 1)
    def _():
        halo_recv[pl.ds(half, half), :] = jnp.zeros((half, deep), BF16)
        back[pl.ds(half, half), :] = jnp.zeros((half, deep), BF16)

    barrier = pltpu.get_barrier_semaphore()

    def greet(k, carry):
        pl.semaphore_signal(
            barrier, inc=1, device_id=(lax.rem(me + k, n),), device_id_type=MESH
        )
        return carry

    lax.fori_loop(1, n, greet, 0)

    index_ref[...] = jnp.zeros_like(index_ref)
    for name, ref in (
        ("enc_source", enc_source_ref),
        ("enc_target", enc_target_ref),
        ("proc_source", proc_source_ref),
        ("proc_target", proc_target_ref),
    ):
        for g in range(ref.shape[1] // LANES):
            index_ref[at[name] + g : at[name] + g + 1, :] = ref[:, g * LANES : (g + 1) * LANES]
    each = half // LANES
    for g in range(2 * each):
        index_ref[at["lists"] + g : at["lists"] + g + 1, :] = lists_ref[
            g // each : g // each + 1, g % each * LANES : (g % each + 1) * LANES
        ]
    for j in range(slots):
        index_ref[at["mesh_lists"] + j : at["mesh_lists"] + j + 1, 0:n] = mesh_lists_ref[
            j : j + 1, :
        ]
    turned = jnp.transpose(index_ref[...])
    for g in range(at["mesh_lists"]):
        column[pl.ds(g * LANES, LANES), :] = jnp.broadcast_to(
            turned[:, g : g + 1], (LANES, LANES)
        )

    def columns(name, start, rows):
        return column[pl.ds(at[name] * LANES + start, rows), :]

    grid_ref[pl.ds(deep - LANES, LANES), :] = jnp.zeros((LANES, grid_count), BF16)
    grid_ref[pl.ds(0, channels), :] = grid_in[...]
    list_hot[...] = pick(columns("lists", 0, 2 * half), 0, grid_count)
    halo_send[...] = nt(list_hot[...], grid_ref[...]).astype(BF16)
    pl.semaphore_wait(barrier, n - 1)
    exchange_start(halo_send, halo_recv, 0)

    w_embed[pl.ds(deep - LANES, LANES), :] = jnp.zeros((LANES, width), BF16)
    w_embed[pl.ds(0, channels), :] = embed_in[...]
    inner = lax.broadcasted_iota(jnp.int32, (n, per, LANES), 1)
    listed = jnp.zeros((n, per, LANES), jnp.int32)
    for j in range(slots):
        g = at["mesh_lists"] + j
        value = jnp.broadcast_to(turned[0:n, g : g + 1], (n, LANES))
        listed = jnp.where(
            lax.shift_right_logical(inner, shift) == j,
            jnp.broadcast_to(value[:, None, :], (n, per, LANES)),
            listed,
        )
    hot_lists[...] = pick(listed.reshape(slabs, LANES), 0, nodes)

    def embed(i, carry):
        rows = pl.ds(pl.multiple_of(i * TILE, TILE), TILE)
        hidden, slope = gate(tn(grid_ref[:, rows], w_embed[...]))
        slope_grid[rows, :] = slope.astype(BF16)
        table[rows, :] = nn(hidden.astype(BF16), w_source[...]).astype(BF16)
        return carry

    lax.fori_loop(0, grid_count // TILE, embed, 0)
    mesh = mesh_ref[...]
    table[pl.ds(grid_count, nodes), :] = nn(mesh, w_target[...]).astype(BF16)

    def enc_own(i, carry):
        start = pl.multiple_of(i * TILE, TILE)
        rows = pl.ds(start, TILE)
        own = pick(columns("enc_target", start, TILE), 0, nodes)
        hot_enc[rows, :] = own
        hot_halo[rows, :] = pick(columns("enc_source", start, TILE), grid_count, 2 * half)
        chosen = jnp.concatenate(
            [pick(columns("enc_source", start, TILE), 0, grid_count), own], axis=1
        )
        pre[rows, :] = nn(chosen, table[...])
        return carry

    lax.fori_loop(0, enc // TILE, enc_own, 0)
    row_enc[...] = spread(index_ref, at["enc_target"], enc // LANES, 0, nodes)
    row_halo[...] = spread(index_ref, at["enc_source"], enc // LANES, grid_count, 2 * half)
    exchange_wait(halo_send, halo_recv, 0)
    hidden, slope = gate(nn(halo_recv[...], w_embed[...]))
    slope_halo[...] = slope.astype(BF16)
    halo[...] = nn(hidden.astype(BF16), w_source[...]).astype(BF16)

    def enc_halo(i, carry):
        rows = pl.ds(pl.multiple_of(i * TILE, TILE), TILE)
        message, slope = gate(pre[rows, :] + nn(hot_halo[rows, :], halo[...]))
        edge[rows, :] = message.astype(BF16)
        slope_enc[rows, :] = slope.astype(BF16)
        return carry

    lax.fori_loop(0, enc // TILE, enc_halo, 0)
    edges = pl.ds(0, enc)
    enc_sum = nn(row_enc[...], edge[edges, :])
    update, slope_node = gate(nn(enc_sum.astype(BF16), w_node[...]))
    latent = (mesh.astype(F32) + update).astype(BF16)
    sender = nn(latent, w_sender[...]).astype(BF16)
    slab_send[...] = (
        packed(nn(hot_lists[...], sender), blocks).reshape(n, per, LANES).astype(BF16)
    )
    scatter_start(slab_send, slab_recv, 0)
    slab_recv[me] = slab_send[me]
    pair[pl.ds(0, nodes), :] = sender
    pair[pl.ds(nodes, nodes), :] = nn(latent, w_receiver[...]).astype(BF16)

    def proc_own(i, carry):
        start = pl.multiple_of(i * TILE, TILE)
        rows = pl.ds(start, TILE)
        own = pick(columns("proc_target", start, TILE), 0, nodes)
        hot_proc[rows, :] = own
        hot_far[rows, :] = pick(columns("proc_source", start, TILE), nodes, slabs, shift)
        chosen = jnp.concatenate(
            [pick(columns("proc_source", start, TILE), 0, nodes), own], axis=1
        )
        pre[rows, :] = nn(chosen, pair[...])
        return carry

    lax.fori_loop(0, proc // TILE, proc_own, 0)
    row_proc[...] = spread(index_ref, at["proc_target"], proc // LANES, 0, nodes)
    row_far[...] = spread(index_ref, at["proc_source"], proc // LANES, nodes, slabs, shift)
    scatter_wait(slab_send, slab_recv, 0)
    arrived = unpacked(slab_recv[...].astype(F32).reshape(slabs, LANES), blocks)

    def proc_far(i, carry):
        rows = pl.ds(pl.multiple_of(i * TILE, TILE), TILE)
        message, slope = gate(pre[rows, :] + nn(hot_far[rows, :], arrived))
        edge[rows, :] = message.astype(BF16)
        slope_proc[rows, :] = slope.astype(BF16)
        return carry

    lax.fori_loop(0, proc // TILE, proc_far, 0)
    proc_sum = nn(row_proc[...], edge[...])
    update, slope = gate(nn(proc_sum.astype(BF16), w_update[...]))
    out_ref[...] = (latent.astype(F32) + update).astype(BF16)
    cotangent = cot_ref[...].astype(F32)
    grad_sum = nt((cotangent * slope).astype(BF16), w_update[...]).astype(BF16)

    def proc_back(i, carry):
        rows = pl.ds(pl.multiple_of(i * TILE, TILE), TILE)
        edge[rows, :] = (
            nn(hot_proc[rows, :], grad_sum) * slope_proc[rows, :].astype(F32)
        ).astype(BF16)
        return carry

    lax.fori_loop(0, proc // TILE, proc_back, 0)
    turn_send[...] = (
        packed(nn(row_far[...], edge[...]), blocks).reshape(n, per, LANES).astype(BF16)
    )
    scatter_start(turn_send, turn_recv, 1)
    turn_recv[me] = turn_send[me]
    grad_receiver = nn(row_proc[...], edge[...]).astype(BF16)
    grad_latent = cotangent + nt(grad_receiver, w_receiver[...])
    grad_sender = nn(spread(index_ref, at["proc_source"], proc // LANES, 0, nodes), edge[...])
    scatter_wait(turn_send, turn_recv, 1)
    grad_sender = grad_sender + tn(
        hot_lists[...], unpacked(turn_recv[...].astype(F32).reshape(slabs, LANES), blocks)
    )
    grad_latent = grad_latent + nt(grad_sender.astype(BF16), w_sender[...])
    grad_latent = grad_latent.astype(BF16).astype(F32)
    grad_sum = nt((grad_latent * slope_node).astype(BF16), w_node[...]).astype(BF16)

    def enc_back(i, carry):
        rows = pl.ds(pl.multiple_of(i * TILE, TILE), TILE)
        edge[rows, :] = (
            nn(hot_enc[rows, :], grad_sum) * slope_enc[rows, :].astype(F32)
        ).astype(BF16)
        return carry

    lax.fori_loop(0, enc // TILE, enc_back, 0)
    grad_far = nt(nn(row_halo[...], edge[edges, :]).astype(BF16), w_source[...])
    grad_far = (grad_far * slope_halo[...].astype(F32)).astype(BF16)
    back_send[...] = nt(grad_far, w_embed[...]).astype(BF16)
    exchange_start(back_send, back, 1)
    grad_target = nn(row_enc[...], edge[edges, :]).astype(BF16)
    grad_mesh_ref[...] = (grad_latent + nt(grad_target, w_target[...])).astype(BF16)

    def grid_own(i, carry):
        start = pl.multiple_of(i * TILE, TILE)
        rows = pl.ds(start, TILE)
        total = nn(spread(index_ref, at["enc_source"], enc // LANES, start, TILE), edge[edges, :])
        grad_hidden = nt(total.astype(BF16), w_source[...])
        grad_pre = (grad_hidden * slope_grid[rows, :].astype(F32)).astype(BF16)
        grad_part[:, rows] = nt(w_embed[...], grad_pre)
        return carry

    lax.fori_loop(0, grid_count // TILE, grid_own, 0)
    exchange_wait(back_send, back, 1)
    total = grad_part[...] + tn(back[...], list_hot[...])
    grad_grid_ref[...] = total[0:channels, :].astype(BF16)


def local(
    grid_input,
    mesh_init,
    cotangent,
    grid_lists,
    encoder_source,
    encoder_target,
    mesh_lists,
    mesh_source,
    mesh_target,
    w_embed,
    w_source,
    w_target,
    w_node,
    w_sender,
    w_receiver,
    w_update,
):
    n = lax.axis_size("band")
    channels, grid_count = grid_input.shape
    nodes, width = mesh_init.shape
    half = grid_lists.shape[1]
    enc = encoder_source.shape[0]
    proc = mesh_source.shape[0]
    slots = mesh_lists.shape[1]
    per = slots * (width // LANES)
    slabs = n * per
    deep = -(-channels // LANES) * LANES
    at = {}
    used = 0
    for name, groups in (
        ("enc_source", enc // LANES),
        ("enc_target", enc // LANES),
        ("proc_source", proc // LANES),
        ("proc_target", proc // LANES),
        ("lists", 2 * half // LANES),
        ("mesh_lists", slots),
    ):
        at[name] = used
        used += groups
    most = max(enc, proc)
    vmem = pl.BlockSpec(memory_space=pltpu.VMEM)
    half_vmem = lambda *shape: pltpu.VMEM(shape, BF16)
    return pl.pallas_call(
        functools.partial(kernel, n, at),
        out_shape=(
            jax.ShapeDtypeStruct((nodes, width), BF16),
            jax.ShapeDtypeStruct((channels, grid_count), BF16),
            jax.ShapeDtypeStruct((nodes, width), BF16),
        ),
        in_specs=[vmem] * 16,
        out_specs=(vmem, vmem, vmem),
        scratch_shapes=[
            pltpu.VMEM((-(-used // 8) * 8, LANES), jnp.int32),
            pltpu.VMEM((used * LANES, LANES), jnp.int32),
            half_vmem(deep, grid_count),
            half_vmem(deep, width),
            half_vmem(2 * half, grid_count),
            half_vmem(grid_count + nodes, width),
            half_vmem(2 * half, width),
            half_vmem(2 * half, deep),
            half_vmem(2 * half, deep),
            half_vmem(2 * half, deep),
            half_vmem(2 * half, deep),
            pltpu.VMEM((most, width), F32),
            half_vmem(most, width),
            pltpu.VMEM((deep, grid_count), F32),
            half_vmem(grid_count, width),
            half_vmem(2 * half, width),
            half_vmem(enc, width),
            half_vmem(proc, width),
            half_vmem(2 * nodes, width),
            half_vmem(enc, 2 * half),
            half_vmem(enc, nodes),
            half_vmem(nodes, enc),
            half_vmem(2 * half, enc),
            half_vmem(proc, slabs),
            half_vmem(proc, nodes),
            half_vmem(nodes, proc),
            half_vmem(slabs, proc),
            half_vmem(slabs, nodes),
            half_vmem(n, per, LANES),
            half_vmem(n, per, LANES),
            half_vmem(n, per, LANES),
            half_vmem(n, per, LANES),
            pltpu.SemaphoreType.DMA((2, 2, 2)),
            pltpu.SemaphoreType.DMA((2, 2)),
        ],
        compiler_params=pltpu.CompilerParams(
            collective_id=0, has_side_effects=True, vmem_limit_bytes=56 * 1024 * 1024
        ),
    )(
        encoder_source.reshape(1, -1),
        encoder_target.reshape(1, -1),
        mesh_source.reshape(1, -1),
        mesh_target.reshape(1, -1),
        grid_lists,
        mesh_lists.T,
        grid_input,
        mesh_init,
        cotangent,
        w_embed,
        w_source,
        w_target,
        w_node,
        w_sender,
        w_receiver,
        w_update,
    )


def solution(mesh):
    placed = (
        P(None, "band"),
        P("band", None),
        P("band", None),
        P("band", None),
        P("band"),
        P("band"),
        P("band", None),
        P("band"),
        P("band"),
        P(),
        P(),
        P(),
        P(),
        P(),
        P(),
        P(),
    )
    return jax.shard_map(
        local,
        mesh=mesh,
        in_specs=placed,
        out_specs=(P("band", None), P(None, "band"), P("band", None)),
        check_vma=False,
    )
```

time: 113 us -> 48.3 us (0.43)
  the two profiles are of different devices: /device:TPU:7 before, /device:TPU:0 now
where the time goes in v2:
time: 48.3 us; the launch traced here: 48.1 us
  Pallas kernels  42 us (87%)
  local copies, waits for them, and re-layouts  5.42 us (11%)
  between operations  0.66 us (1%)
    pallas_call x1, Pallas kernels, local(): pl.pallas_call(functools.partial(kernel, n, at), out_shape=(jax.ShapeDtyp...  42 us
    unnamed x9, local copies, waits for them, and re-layouts  3.53 us
    reshape x1, local copies, waits for them, and re-layouts, local(): encoder_source.reshape(1, -1)  1.3 us

profile of v2, /device:TPU:0, one launch (start us, length us, event | category | flops | bytes accessed | tf_op | source)
XLA Modules:
  0.0 48.1 jit_solution(6898647683574487468)
XLA Ops:
  0.6 0.0 copy-start.2
  0.6 1.3 %reshape.18.enc_source_ref = s32[1,1536]{1,0:T(1,128)} reshape(s32[1536]{0:T(1024)} %param.20) | data formatting | bytes 12288 | tf_op jit(solution)/shard_map/reshape | solution.py:493
  1.9 0.0 copy-done.2
  1.9 0.6 %reshape.19.enc_target_ref = s32[1,1536]{1,0:T(1,128)} reshape(s32[1536]{0:T(1024)S(1)} %copy-done.2) | data formatting | bytes 12288 | tf_op jit(solution)/shard_map/reshape | solution.py:494
  2.5 42.0 %shard_map.175 = (bf16[256,512]{1,0:T(8,128)(2,1)}, bf16[227,1024]{1,0:T(8,128)(2,1)}, bf16[256,512]{1,0:T(8,128)(2,1)}) custom-call(s32[1,1536]{1,0:T(1,128)} %reshape.18.enc_source_ref, s32[1,1536]{1,0:T(1,128)} %reshape.19.enc_target_ref, s32[1,2048]{1,0:T(1,128)} %bitcast.3, s32[1,2048]{1,0:T(1,128)} %bitcast.4, s32[2,256]{1,0:T(2,128)} %lists_ref.1, ...), custom_call_target="tpu_custom_call" | custom-call | tf_op jit(solution)/shard_map/pallas_call | solution.py:444
  44.6 0.0 copy-start
  44.6 1.7 %copy.22 = bf16[256,512]{1,0:T(8,128)(2,1)} copy(bf16[256,512]{1,0:T(8,128)(2,1)} %get-tuple-element.6) | data formatting | bytes 524288
  46.3 0.0 copy-done
  46.3 0.0 copy-start.1
  46.3 0.8 %copy.23 = bf16[227,1024]{1,0:T(8,128)(2,1)} copy(bf16[227,1024]{1,0:T(8,128)(2,1)S(1)} %copy-done) | data formatting | bytes 929792
  47.1 0.3 copy-done.1
  47.4 0.7 %copy.24 = bf16[256,512]{1,0:T(8,128)(2,1)} copy(bf16[256,512]{1,0:T(8,128)(2,1)S(1)} %copy-done.1) | data formatting | bytes 524288
Async XLA Ops:
  0.6 1.3 %copy-start.2 = (s32[1536]{0:T(1024)S(1)}, s32[1536]{0:T(1024)}, u32[]{:S(2)}) copy-start(s32[1536]{0:T(1024)} %param.21) | copy-start | bytes 18436
  44.6 1.7 %copy-start = (bf16[227,1024]{1,0:T(8,128)(2,1)S(1)}, bf16[227,1024]{1,0:T(8,128)(2,1)}, u32[]{:S(2)}) copy-start(bf16[227,1024]{1,0:T(8,128)(2,1)} %get-tuple-element.7) | copy-start | bytes 1394692
  46.3 1.1 %copy-start.1 = (bf16[256,512]{1,0:T(8,128)(2,1)S(1)}, bf16[256,512]{1,0:T(8,128)(2,1)}, u32[]{:S(2)}) copy-start(bf16[256,512]{1,0:T(8,128)(2,1)} %get-tuple-element.8) | copy-start | bytes 786436

commit v3 on v2

--- a/solution.py
+++ b/solution.py
@@ -219,8 +219,10 @@
         ("proc_source", proc_source_ref),
         ("proc_target", proc_target_ref),
     ):
-        for g in range(ref.shape[1] // LANES):
-            index_ref[at[name] + g : at[name] + g + 1, :] = ref[:, g * LANES : (g + 1) * LANES]
+        for g in range(ref.shape[0] // LANES):
+            index_ref[at[name] + g : at[name] + g + 1, :] = ref[pl.ds(g * LANES, LANES)].reshape(
+                1, LANES
+            )
     each = half // LANES
     for g in range(2 * each):
         index_ref[at["lists"] + g : at["lists"] + g + 1, :] = lists_ref[
@@ -396,6 +398,12 @@
     exchange_wait(back_send, back, 1)
     total = grad_part[...] + tn(back[...], list_hot[...])
     grad_grid_ref[...] = total[0:channels, :].astype(BF16)
+
+
+def hand_over(first, second, third, first_out, second_out, third_out):
+    first_out[...] = first[...]
+    second_out[...] = second[...]
+    third_out[...] = third[...]
 
 
 def local(
@@ -441,7 +449,7 @@
     most = max(enc, proc)
     vmem = pl.BlockSpec(memory_space=pltpu.VMEM)
     half_vmem = lambda *shape: pltpu.VMEM(shape, BF16)
-    return pl.pallas_call(
+    results = pl.pallas_call(
         functools.partial(kernel, n, at),
         out_shape=(
             jax.ShapeDtypeStruct((nodes, width), BF16),
@@ -490,10 +498,10 @@
             collective_id=0, has_side_effects=True, vmem_limit_bytes=56 * 1024 * 1024
         ),
     )(
-        encoder_source.reshape(1, -1),
-        encoder_target.reshape(1, -1),
-        mesh_source.reshape(1, -1),
-        mesh_target.reshape(1, -1),
+        encoder_source,
+        encoder_target,
+        mesh_source,
+        mesh_target,
         grid_lists,
         mesh_lists.T,
         grid_input,
@@ -507,6 +515,12 @@
         w_receiver,
         w_update,
     )
+    return pl.pallas_call(
+        hand_over,
+        out_shape=tuple(jax.ShapeDtypeStruct(r.shape, r.dtype) for r in results),
+        in_specs=[vmem] * 3,
+        out_specs=(vmem, vmem, vmem),
+    )(*results)
 
 
 def solution(mesh):

time: 48.3 us -> 45 us (0.932)
  local copies, waits for them, and re-layouts: 5.42 us -> 0 us
  Pallas kernels: 42 us -> 44.2 us
    unnamed x9 -> x0, local copies, waits for them, and re-layouts: 3.53 us -> none
    pallas_call x0 -> x1, Pallas kernels: none -> 2.15 us  [local(): pl.pallas_call(hand_over, out_shape=tuple((jax.ShapeDtypeStruct(r.shape,...]
    reshape x2 -> x0, local copies, waits for them, and re-layouts: 1.9 us -> none  [the longest x1 1.3 us: local(): encoder_source.reshape(1, -1)]
where the time goes in v3:
time: 45 us; the launch traced here: 44.8 us
  Pallas kernels  44.2 us (98%)
  between operations  0.65 us (1%)
    pallas_call x1, Pallas kernels, local(): pl.pallas_call(functools.partial(kernel, n, at), out_shape=(jax.ShapeDtyp...  42 us
    pallas_call x1, Pallas kernels, local(): pl.pallas_call(hand_over, out_shape=tuple((jax.ShapeDtypeStruct(r.shape,...  2.15 us

profile of v3, /device:TPU:0, one launch (start us, length us, event | category | flops | bytes accessed | tf_op | source)
XLA Modules:
  0.0 44.8 jit_solution(4599119193970517321)
XLA Ops:
  0.6 42.0 %shard_map.175 = (bf16[256,512]{1,0:T(8,128)(2,1)}, bf16[227,1024]{1,0:T(8,128)(2,1)}, bf16[256,512]{1,0:T(8,128)(2,1)}) custom-call(s32[1536]{0:T(1024)} %enc_source_ref.1, s32[1536]{0:T(1024)} %enc_target_ref.1, s32[2048]{0:T(1024)} %proc_source_ref.1, s32[2048]{0:T(1024)} %proc_target_ref.1, s32[2,256]{1,0:T(2,128)} %lists_ref.1, s32[2,32]{1,0:T(2,128)} %bitcast.1, ...), custom_call_target="tpu_custom_call" | custom-call | tf_op jit(solution)/shard_map/pallas_call | solution.py:452
  42.7 2.2 %shard_map.176 = (bf16[256,512]{1,0:T(8,128)(2,1)}, bf16[227,1024]{1,0:T(8,128)(2,1)}, bf16[256,512]{1,0:T(8,128)(2,1)}) custom-call(bf16[256,512]{1,0:T(8,128)(2,1)} %get-tuple-element.6.first, bf16[227,1024]{1,0:T(8,128)(2,1)} %get-tuple-element.7.second, bf16[256,512]{1,0:T(8,128)(2,1)} %get-tuple-element.8.third), custom_call_target="tpu_custom_call" | custom-call | tf_op jit(solution)/shard_map/pallas_call | solution.py:518
